TPU v7x, 32 devices: a whole 2x2x4 slice. The times are simulated.
32 devices in a mesh: seq: 8 (over z, y), head: 4 (over x, core).
Axes of the slice: x: 2, y: 2, z: 4, core: 2. Of those that a mesh axis runs over, the one named last changes fastest.
Arguments:
- block_input: bfloat16 [4096, 1024], P('seq'), may hold values from -6 to 6
- norm1_gain: bfloat16 [1024], replicated, may hold values from 0.5 to 1.5
- w_query: bfloat16 [1024, 1024], P(None, 'head'), may hold values from -0.1875 to 0.1875
- w_key: bfloat16 [1024, 1024], P(None, 'head'), may hold values from -0.1875 to 0.1875
- w_value: bfloat16 [1024, 2048], P(None, 'head'), may hold values from -0.1875 to 0.1875
- w_gate: bfloat16 [1024, 2048], P(None, 'head'), may hold values from -0.1875 to 0.1875
- w_decay: bfloat16 [1024, 8], P(None, 'head'), may hold values from -0.1875 to 0.1875
- w_beta: bfloat16 [1024, 8], P(None, 'head'), may hold values from -0.1875 to 0.1875
- conv_query: bfloat16 [4, 1024], P(None, 'head'), may hold values from -3 to 3
- conv_key: bfloat16 [4, 1024], P(None, 'head'), may hold values from -3 to 3
- conv_value: bfloat16 [4, 2048], P(None, 'head'), may hold values from -3 to 3
- decay_rate: float32 [8], P('head'), may hold values from 4.8828126e-05 to 0.08
- out_gain: bfloat16 [256], replicated, may hold values from 0.5 to 1.5
- w_out: bfloat16 [2048, 1024], P('head'), may hold values from -0.25 to 0.25
- norm2_gain: bfloat16 [1024], replicated, may hold values from 0.5 to 1.5
- w_ffn_gate: bfloat16 [1024, 2816], P(None, 'head'), may hold values from -0.1875 to 0.1875
- w_ffn_up: bfloat16 [1024, 2816], P(None, 'head'), may hold values from -0.1875 to 0.1875
- w_ffn_down: bfloat16 [2816, 1024], P('head'), may hold values from -0.21875 to 0.21875
- cotangent: bfloat16 [4096, 1024], P('seq'), may hold values from -6 to 6
Outputs:
- out: bfloat16 [4096, 1024], P('seq')
- d_block_input: float32 [4096, 1024], P('seq')
- d_norm1_gain: float32 [1024], P('seq')
- d_w_query: float32 [1024, 1024], P('seq', 'head')
- d_w_key: float32 [1024, 1024], P('seq', 'head')
- d_w_value: float32 [1024, 2048], P('seq', 'head')
- gate_weight_gradient: float32 [1024, 2048], P('seq', 'head')
- d_w_decay: float32 [1024, 8], P('seq', 'head')
- d_w_beta: float32 [1024, 8], P('seq', 'head')
- d_conv_query: float32 [4, 1024], P(None, 'head')
- d_conv_key: float32 [4, 1024], P(None, 'head')
- d_conv_value: float32 [4, 2048], P(None, 'head')
- d_decay_rate: float32 [8], P('head')
- d_out_gain: float32 [256], P('seq')
- d_w_out: float32 [2048, 1024], P('head', 'seq')
- d_norm2_gain: float32 [1024], P('seq')
- d_w_ffn_gate: float32 [1024, 2816], P('seq', 'head')
- d_w_ffn_up: float32 [1024, 2816], P('seq', 'head')
- d_w_ffn_down: float32 [2816, 1024], P('head', 'seq')
All inputs are finite; a program needn't handle non-finite values.
Results may differ from a plain program's by a relative error of at most 0.033.
Values may be sent and summed in bfloat16 or wider, within the bound.
No kernel may reach another device: no remote copies, remote signals or barrier semaphores. Data moves between devices by JAX's collectives and lax.ppermute only.
A program may use at most 192 MiB of HBM per device.

v0:
```python
import jax
import jax.numpy as jnp
from jax import lax
from jax.sharding import PartitionSpec as P

KEY = 128
VALUE = 256
GROUP = 64


highest_precision = lax.Precision.HIGHEST
epsilon = 1e-06


def from_behind(block, axis, distance):
    devices = range(lax.axis_size(axis))
    route = [(i - distance, i) for i in devices if i - distance in devices]
    return lax.ppermute(block, axis, route)


def matmul_bf(first_operand, second_operand):
    return jnp.dot(first_operand, second_operand, preferred_element_type=jnp.float32)


def inner_rows(first_operand, second_operand):
    return lax.dot_general(
        first_operand, second_operand, (((0,), (0,)), ((), ())), preferred_element_type=jnp.float32
    )


def against_rows(first_operand, second_operand):
    return lax.dot_general(
        first_operand, second_operand, (((1,), (1,)), ((), ())), preferred_element_type=jnp.float32
    )


def round_trip(values):
    return lax.optimization_barrier(values.astype(jnp.bfloat16)).astype(jnp.float32)


def row_norm(values, gain_vec):
    return (
        values * lax.rsqrt(jnp.mean(values * values, axis=-1, keepdims=True) + epsilon) * gain_vec
    )


def unit_rows(values, scale_factor):
    return (
        values
        * lax.rsqrt(jnp.sum(values * values, axis=-1, keepdims=True) + epsilon)
        * scale_factor
    )


def mixer_inputs(extended, conv_taps, decay_pre, beta_pre, decay_rate):
    length, head_count = decay_pre.shape
    tap_reach = conv_taps.shape[0] - 1
    summed = conv_taps[0] * extended[tap_reach:]
    for offset in range(1, conv_taps.shape[0]):
        summed = (
            summed + conv_taps[offset] * extended[tap_reach - offset : tap_reach - offset + length]
        )
    active = jax.nn.silu(summed)
    key_cols = head_count * KEY
    queries = unit_rows(active[:, :key_cols].reshape(length, head_count, KEY), KEY ** (-0.5))
    keys_act = unit_rows(active[:, key_cols : 2 * key_cols].reshape(length, head_count, KEY), 1.0)
    values_act = active[:, 2 * key_cols :].reshape(length, head_count, VALUE)
    log_decay = -decay_rate * jax.nn.softplus(decay_pre)
    beta_gate = jax.nn.sigmoid(beta_pre)
    return (queries, keys_act, values_act, log_decay, beta_gate)


def group_parts(keys_act, values_act, log_decay, beta_gate):
    length, head_count = log_decay.shape
    blocks = length // GROUP
    keys_c = keys_act.reshape(blocks, GROUP, head_count, KEY)
    values_c = values_act.reshape(blocks, GROUP, head_count, VALUE)
    decay_c = log_decay.reshape(blocks, GROUP, head_count)
    beta_c = jnp.transpose(beta_gate.reshape(blocks, GROUP, head_count), (0, 2, 1))
    places = jnp.arange(GROUP)
    inclusive = (places[:, None] >= places[None, :]).astype(jnp.float32)
    strict = (places[:, None] > places[None, :]).astype(jnp.float32)
    cumulative = jnp.einsum("ij,njh->nhi", inclusive, decay_c, precision=highest_precision)
    spread = cumulative[..., :, None] - cumulative[..., None, :]
    decay_mat = jnp.exp(jnp.where(inclusive > 0, spread, 0.0)) * inclusive
    key_key = jnp.einsum("nihk,njhk->nhij", keys_c, keys_c, precision=highest_precision)
    system = jnp.eye(GROUP, dtype=jnp.float32) + beta_c[..., :, None] * decay_mat * key_key * strict
    growth = jnp.exp(cumulative)
    scaled_values = jnp.einsum("nhc,nchv->nhcv", beta_c, values_c, precision=highest_precision)
    scaled_keys = jnp.einsum("nhc,nchk->nhck", beta_c * growth, keys_c, precision=highest_precision)
    solved_values = lax.linalg.triangular_solve(
        system, scaled_values, left_side=True, lower=True, unit_diagonal=True
    )
    solved_keys = lax.linalg.triangular_solve(
        system, scaled_keys, left_side=True, lower=True, unit_diagonal=True
    )
    tail_decay = jnp.exp(cumulative[..., -1:] - cumulative)
    keys_tail = jnp.einsum("nhc,nchk->nhck", tail_decay, keys_c, precision=highest_precision)
    final_growth = growth[..., -1]
    transfer = final_growth[..., None, None] * jnp.eye(KEY, dtype=jnp.float32) - jnp.einsum(
        "nhck,nhcl->nhkl", keys_tail, solved_keys, precision=highest_precision
    )
    offset_state = jnp.einsum(
        "nhck,nhcv->nhkv", keys_tail, solved_values, precision=highest_precision
    )
    return (keys_c, decay_mat, growth, solved_values, solved_keys, transfer, offset_state)


def compose_maps(earlier, latter_map):
    joined = jnp.einsum("hij,hjk->hik", latter_map[0], earlier[0], precision=highest_precision)
    shifted = (
        jnp.einsum("hij,hjk->hik", latter_map[0], earlier[1], precision=highest_precision)
        + latter_map[1]
    )
    return (joined, shifted)


def identity_map(head_count):
    eye_stack = jnp.broadcast_to(jnp.eye(KEY, dtype=jnp.float32), (head_count, KEY, KEY))
    return (eye_stack, jnp.zeros((head_count, KEY, VALUE), jnp.float32))


def fold_maps(transfers, offsets, head_count):

    def fold_step(composite, table_entries):
        return (compose_maps(composite, table_entries), None)

    composite, unused = lax.scan(fold_step, identity_map(head_count), (transfers, offsets))
    return composite


def run_mixer(queries, parts, state_in):
    keys_c, decay_mat, growth, solved_values, solved_keys, transfer, offset_state = parts
    blocks, head_count = (growth.shape[0], growth.shape[1])
    length = blocks * GROUP
    queries_c = queries.reshape(blocks, GROUP, head_count, KEY)

    def carry_step(incoming_state, table_entries):
        following = (
            jnp.einsum(
                "hij,hjv->hiv", table_entries[0], incoming_state, precision=highest_precision
            )
            + table_entries[1]
        )
        return (following, incoming_state)

    state_out, starts = lax.scan(carry_step, state_in, (transfer, offset_state))
    corrected = solved_values - jnp.einsum(
        "nhck,nhkv->nhcv", solved_keys, starts, precision=highest_precision
    )
    query_key = (
        jnp.einsum("nihk,njhk->nhij", queries_c, keys_c, precision=highest_precision) * decay_mat
    )
    carried = jnp.einsum("nchk,nhkv->nchv", queries_c, starts, precision=highest_precision)
    carried = carried * jnp.transpose(growth, (0, 2, 1))[..., None]
    local_part = jnp.einsum("nhij,nhjv->nihv", query_key, corrected, precision=highest_precision)
    return ((carried + local_part).reshape(length, head_count, VALUE), state_out)


def start_gradient(queries, parts, grad_mixed):
    keys_c, decay_mat, growth, solved_values, solved_keys, transfer, offset_state = parts
    blocks, head_count = (growth.shape[0], growth.shape[1])
    queries_c = queries.reshape(blocks, GROUP, head_count, KEY)
    grad_c = grad_mixed.reshape(blocks, GROUP, head_count, VALUE)
    grown = grad_c * jnp.transpose(growth, (0, 2, 1))[..., None]
    from_carried = jnp.einsum("nchk,nchv->nhkv", queries_c, grown, precision=highest_precision)
    query_key = (
        jnp.einsum("nihk,njhk->nhij", queries_c, keys_c, precision=highest_precision) * decay_mat
    )
    grad_corrected = jnp.einsum("nhij,nihv->nhjv", query_key, grad_c, precision=highest_precision)
    grad_starts = from_carried - jnp.einsum(
        "nhck,nhcv->nhkv", solved_keys, grad_corrected, precision=highest_precision
    )

    def back_step(pending, table_entries):
        earlier = table_entries[1] + jnp.einsum(
            "hji,hjv->hiv", table_entries[0], pending, precision=highest_precision
        )
        return (earlier, None)

    initial = jnp.zeros((head_count, KEY, VALUE), jnp.float32)
    direct, unused = lax.scan(back_step, initial, (transfer, grad_starts), reverse=True)
    return direct


def gate_norm(mixed, gate_pre, gain_vec):
    length, head_count = (mixed.shape[0], mixed.shape[1])
    gate_view = gate_pre.reshape(length, head_count, VALUE)
    return (row_norm(mixed, gain_vec) * jax.nn.silu(gate_view)).reshape(length, head_count * VALUE)


def swiglu(gate_in, up_in):
    return jax.nn.silu(gate_in) * up_in


def per_device(
    block_input,
    norm1_gain,
    w_query,
    w_key,
    w_value,
    w_gate,
    w_decay,
    w_beta,
    conv_query,
    conv_key,
    conv_value,
    decay_rate,
    out_gain,
    w_out,
    norm2_gain,
    w_ffn_gate,
    w_ffn_up,
    w_ffn_down,
    cotangent,
):
    length = block_input.shape[0]
    head_count = w_decay.shape[1]
    key_cols = w_query.shape[1]
    tap_reach = conv_query.shape[0] - 1
    inputs32 = block_input.astype(jnp.float32)
    normed32, norm1_back = jax.vjp(row_norm, inputs32, norm1_gain.astype(jnp.float32))
    normed = normed32.astype(jnp.bfloat16)
    query_pre = matmul_bf(normed, w_query).astype(jnp.bfloat16)
    key_pre = matmul_bf(normed, w_key).astype(jnp.bfloat16)
    value_pre = matmul_bf(normed, w_value).astype(jnp.bfloat16)
    gate_pre = matmul_bf(normed, w_gate)
    decay_pre = matmul_bf(normed, w_decay)
    beta_pre = matmul_bf(normed, w_beta)
    stacked = jnp.concatenate([query_pre, key_pre, value_pre], axis=1)
    edge_rows = from_behind(stacked[length - tap_reach :], "seq", 1)
    extended = jnp.concatenate([edge_rows, stacked], axis=0).astype(jnp.float32)
    conv_taps = jnp.concatenate([conv_query, conv_key, conv_value], axis=1).astype(jnp.float32)
    prepared, prepare_back = jax.vjp(
        mixer_inputs, extended, conv_taps, decay_pre, beta_pre, decay_rate
    )
    queries = round_trip(prepared[0])
    keys_act = round_trip(prepared[1])
    values_act = round_trip(prepared[2])
    log_decay, beta_gate = (prepared[3], prepared[4])
    parts, parts_back = jax.vjp(group_parts, keys_act, values_act, log_decay, beta_gate)
    transfer, offset_state = fold_maps(parts[5], parts[6], head_count)

    def relay_step(turn_index, incoming_state):
        following = (
            jnp.einsum("hij,hjv->hiv", transfer, incoming_state, precision=highest_precision)
            + offset_state
        )
        return from_behind(following.astype(jnp.bfloat16), "seq", 1).astype(following.dtype)

    state_in = lax.fori_loop(0, lax.axis_size("seq") - 1, relay_step, jnp.zeros_like(offset_state))
    mixer_result, mixer_back = jax.vjp(run_mixer, queries, parts, state_in)
    gated32, gate_back = jax.vjp(gate_norm, mixer_result[0], gate_pre, out_gain.astype(jnp.float32))
    gated = gated32.astype(jnp.bfloat16)
    branch = lax.psum(matmul_bf(gated, w_out).astype(jnp.bfloat16), "head").astype(jnp.float32)
    middle = inputs32 + branch
    normed2_32, norm2_back = jax.vjp(row_norm, middle, norm2_gain.astype(jnp.float32))
    normed2 = normed2_32.astype(jnp.bfloat16)
    ffn_gate = matmul_bf(normed2, w_ffn_gate)
    ffn_up = matmul_bf(normed2, w_ffn_up)
    hidden32, swiglu_back = jax.vjp(swiglu, ffn_gate, ffn_up)
    hidden = hidden32.astype(jnp.bfloat16)
    ffn_out = lax.psum(matmul_bf(hidden, w_ffn_down).astype(jnp.bfloat16), "head").astype(
        jnp.float32
    )
    layer_out = (middle + ffn_out).astype(jnp.bfloat16)
    grad_down = inner_rows(hidden, cotangent)
    grad_hidden = against_rows(cotangent, w_ffn_down)
    grad_fgate, grad_fup = swiglu_back(grad_hidden)
    grad_fgate = grad_fgate.astype(jnp.bfloat16)
    grad_fup = grad_fup.astype(jnp.bfloat16)
    grad_wfg = inner_rows(normed2, grad_fgate)
    grad_wfu = inner_rows(normed2, grad_fup)
    grad_normed2 = lax.psum(
        (against_rows(grad_fgate, w_ffn_gate) + against_rows(grad_fup, w_ffn_up)).astype(
            jnp.bfloat16
        ),
        "head",
    ).astype(jnp.float32)
    grad_middle_n, grad_gain2 = norm2_back(grad_normed2)
    grad_middle = cotangent.astype(jnp.float32) + grad_middle_n
    grad_branch = grad_middle.astype(jnp.bfloat16)
    grad_wout = inner_rows(gated, grad_branch)
    grad_gated = against_rows(grad_branch, w_out)
    grad_mixed, grad_gate_pre, grad_outgain = gate_back(grad_gated)
    direct = start_gradient(queries, parts, grad_mixed)
    flipped = jnp.swapaxes(transfer, 1, 2)

    def relay_back(turn_index, pending):
        following = (
            jnp.einsum("hij,hjv->hiv", flipped, pending, precision=highest_precision) + direct
        )
        return from_behind(following.astype(jnp.bfloat16), "seq", -1).astype(following.dtype)

    grad_state = lax.fori_loop(0, lax.axis_size("seq") - 1, relay_back, jnp.zeros_like(direct))
    grad_q, grad_parts, unused = mixer_back((grad_mixed, grad_state))
    grad_k, grad_v, grad_log, grad_beta = parts_back(grad_parts)
    grad_ext, grad_taps, grad_decay_pre, grad_beta_pre, grad_rate = prepare_back(
        (grad_q, grad_k, grad_v, grad_log, grad_beta)
    )
    remote = from_behind(grad_ext[:tap_reach], "seq", -1)
    padding = jnp.zeros((length - tap_reach, grad_ext.shape[1]), jnp.float32)
    grad_stacked = (grad_ext[tap_reach:] + jnp.concatenate([padding, remote], axis=0)).astype(
        jnp.bfloat16
    )
    grad_qp = grad_stacked[:, :key_cols]
    grad_kp = grad_stacked[:, key_cols : 2 * key_cols]
    grad_vp = grad_stacked[:, 2 * key_cols :]
    grad_gp = grad_gate_pre.astype(jnp.bfloat16)
    grad_dp = grad_decay_pre.astype(jnp.bfloat16)
    grad_bp = grad_beta_pre.astype(jnp.bfloat16)
    grad_wq = inner_rows(normed, grad_qp)
    grad_wk = inner_rows(normed, grad_kp)
    grad_wv = inner_rows(normed, grad_vp)
    grad_wg = inner_rows(normed, grad_gp)
    grad_wd = inner_rows(normed, grad_dp)
    grad_wb = inner_rows(normed, grad_bp)
    grad_normed_part = (
        against_rows(grad_qp, w_query)
        + against_rows(grad_kp, w_key)
        + against_rows(grad_vp, w_value)
        + against_rows(grad_gp, w_gate)
        + against_rows(grad_dp, w_decay)
        + against_rows(grad_bp, w_beta)
    )
    grad_normed, grad_outgain_all = (
        lax.psum(grad_normed_part.astype(jnp.bfloat16), "head").astype(jnp.float32),
        lax.psum(grad_outgain.astype(jnp.bfloat16), "head").astype(jnp.float32),
    )
    grad_input_n, grad_gain1 = norm1_back(grad_normed)
    grad_input = grad_middle + grad_input_n
    small_sums = lax.psum((grad_taps, grad_rate), "seq")
    combined = (
        lax.psum_scatter(
            grad_gain1.astype(jnp.bfloat16), "seq", scatter_dimension=0, tiled=True
        ).astype(jnp.float32),
        lax.psum_scatter(
            grad_wq.astype(jnp.bfloat16), "seq", scatter_dimension=0, tiled=True
        ).astype(jnp.float32),
        lax.psum_scatter(
            grad_wk.astype(jnp.bfloat16), "seq", scatter_dimension=0, tiled=True
        ).astype(jnp.float32),
        lax.psum_scatter(
            grad_wv.astype(jnp.bfloat16), "seq", scatter_dimension=0, tiled=True
        ).astype(jnp.float32),
        lax.psum_scatter(
            grad_wg.astype(jnp.bfloat16), "seq", scatter_dimension=0, tiled=True
        ).astype(jnp.float32),
        lax.psum_scatter(
            grad_wd.astype(jnp.bfloat16), "seq", scatter_dimension=0, tiled=True
        ).astype(jnp.float32),
        lax.psum_scatter(
            grad_wb.astype(jnp.bfloat16), "seq", scatter_dimension=0, tiled=True
        ).astype(jnp.float32),
        lax.psum_scatter(
            grad_outgain_all.astype(jnp.bfloat16), "seq", scatter_dimension=0, tiled=True
        ).astype(jnp.float32),
        lax.psum_scatter(
            grad_wout.astype(jnp.bfloat16), "seq", scatter_dimension=1, tiled=True
        ).astype(jnp.float32),
        lax.psum_scatter(
            grad_gain2.astype(jnp.bfloat16), "seq", scatter_dimension=0, tiled=True
        ).astype(jnp.float32),
        lax.psum_scatter(
            grad_wfg.astype(jnp.bfloat16), "seq", scatter_dimension=0, tiled=True
        ).astype(jnp.float32),
        lax.psum_scatter(
            grad_wfu.astype(jnp.bfloat16), "seq", scatter_dimension=0, tiled=True
        ).astype(jnp.float32),
        lax.psum_scatter(
            grad_down.astype(jnp.bfloat16), "seq", scatter_dimension=1, tiled=True
        ).astype(jnp.float32),
    )
    mixer_part = combined[:9]
    ffn_part = combined[9:]
    taps_sum = small_sums[0]
    return (
        layer_out,
        grad_input,
        mixer_part[0],
        mixer_part[1],
        mixer_part[2],
        mixer_part[3],
        mixer_part[4],
        mixer_part[5],
        mixer_part[6],
        taps_sum[:, :key_cols],
        taps_sum[:, key_cols : 2 * key_cols],
        taps_sum[:, 2 * key_cols :],
        small_sums[1],
        mixer_part[7],
        mixer_part[8],
        ffn_part[0],
        ffn_part[1],
        ffn_part[2],
        ffn_part[3],
    )


def solution(mesh):
    return jax.shard_map(
        per_device,
        mesh=mesh,
        in_specs=(
            P("seq", None),
            P(),
            P(None, "head"),
            P(None, "head"),
            P(None, "head"),
            P(None, "head"),
            P(None, "head"),
            P(None, "head"),
            P(None, "head"),
            P(None, "head"),
            P(None, "head"),
            P("head"),
            P(),
            P("head", None),
            P(),
            P(None, "head"),
            P(None, "head"),
            P("head", None),
            P("seq", None),
        ),
        out_specs=(
            P("seq", None),
            P("seq", None),
            P("seq"),
            P("seq", "head"),
            P("seq", "head"),
            P("seq", "head"),
            P("seq", "head"),
            P("seq", "head"),
            P("seq", "head"),
            P(None, "head"),
            P(None, "head"),
            P(None, "head"),
            P("head"),
            P("seq"),
            P("head", "seq"),
            P("seq"),
            P("seq", "head"),
            P("seq", "head"),
            P("head", "seq"),
        ),
        check_vma=False,
    )
```

profile of v0, /device:TPU:0, one launch (start us, length us, event | category | flops | bytes accessed | tf_op | source)
XLA Modules:
  0.0 1294.9 jit_solution(7209608571210859601)
XLA Ops:
  14.6 5.6 collective-permute-start.2
  28.1 4.0 fusion.53
  38.5 79.4 %custom-call.12 = f32[8,2,1,64,64]{3,4,2,1,0:T(8,128)S(1)} custom-call(f32[8,2,1,64,64]{4,3,2,1,0:T(8,128)} %add_bitcast_fusion), custom_call_target="InvertDiagBlocksLowerTriangular" | custom-call | tf_op jit(solution)/shard_map/jvp()/triangular_solve | solution.py:94
  131.7 21.3 %while.82 = (s32[]{:T(128)}, f32[2,128,128]{2,1,0:T(8,128)S(1)}, f32[2,128,256]{2,1,0:T(8,128)S(1)}, f32[8,2,128,128]{3,2,1,0:T(8,128)}, f32[8,2,128,256]{3,2,1,0:T(8,128)}, /*index=5*/s32[]{:T(128)}, s32[]{:T(128)}) while((s32[]{:T(128)}, f32[2,128,128]{2,1,0:T(8,128)S(1)}, f32[2,128,256]{2,1,0:T(8,128)S(1)}, ...), condition=%wide.region_3.4_spmd.clone, body=%wide.region_2.3_spmd.clone.sunk | while | flops 151126016 | bytes 2098775 | solution.py:128
  152.9 56.1 %while.83 = (s32[]{:T(128)}, f32[2,128,256]{2,1,0:T(8,128)S(1)}, f32[2,128,128]{2,1,0:T(8,128)S(1)}, f32[2,128,256]{2,1,0:T(8,128)S(1)}, s32[]{:T(128)}, /*index=5*/s32[]{:T(128)}) while((s32[]{:T(128)}, f32[2,128,256]{2,1,0:T(8,128)S(1)}, f32[2,128,128]{2,1,0:T(8,128)S(1)}, f32[2,128,256]{2,1,0:T(8,128)S(1)}, s32[]{:T(128)}, ...), condition=%wide.region_5.6_spmd.clone, body=%wide.region_4.5_spmd.clone.sunk | while | flops 100925440 | bytes 1704055 | solution.py:251
  153.3 3.4 collective-permute-start
  159.6 4.4 collective-permute-start
  166.9 5.2 collective-permute-start
  175.1 5.3 collective-permute-start
  183.2 5.3 collective-permute-start
  192.1 5.6 collective-permute-start
  201.5 5.0 collective-permute-start
  210.6 24.8 %while.80 = (s32[]{:T(128)}, f32[2,128,256]{2,1,0:T(8,128)}, f32[8,2,128,256]{3,2,1,0:T(8,128)S(1)}, f32[8,2,128,128]{3,2,1,0:T(8,128)}, f32[8,2,128,256]{3,2,1,0:T(8,128)}, /*index=5*/s32[]{:T(128)}) while((s32[]{:T(128)}, f32[2,128,256]{2,1,0:T(8,128)}, f32[8,2,128,256]{3,2,1,0:T(8,128)S(1)}, f32[8,2,128,128]{3,2,1,0:T(8,128)}, ...), condition=%wide.region_7.8_spmd, body=%wide.region_6.7_spmd.sunk | while | flops 100728832 | bytes 1967177 | solution.py:147
  257.6 38.9 %all-reduce.24.cloned.1.call-done = bf16[512,1024]{1,0:T(8,128)(2,1)} async-done(((bf16[512,1024]{1,0:T(8,128)(2,1)}), bf16[512,1024]{1,0:T(8,128)(2,1)}) %all-reduce.24.cloned.1.call-update) | async-done | bytes 1048592 | tf_op jit(solution)/shard_map/psum | solution.py:255
  324.9 20.8 %all-reduce.26.cloned.1.call-done = bf16[512,1024]{1,0:T(8,128)(2,1)} async-done(((bf16[512,1024]{1,0:T(8,128)(2,1)}), bf16[512,1024]{1,0:T(8,128)(2,1)}) %all-reduce.26.cloned.1.call-update) | async-done | bytes 1048592 | tf_op jit(solution)/shard_map/psum | solution.py:274
  345.7 3.5 fusion.44
  349.3 5.0 fusion.73
  369.5 3.4 convolution_add_fusion.6
  372.9 3.4 convolution_subtract_fusion
  376.3 11.7 while.84
  388.0 79.3 %while.85 = (s32[]{:T(128)}, f32[2,128,256]{2,1,0:T(8,128)}, f32[2,128,128]{2,1,0:T(8,128)S(1)}, f32[2,128,256]{2,1,0:T(8,128)S(1)}, s32[]{:T(128)}, /*index=5*/s32[]{:T(128)}) while((s32[]{:T(128)}, f32[2,128,256]{2,1,0:T(8,128)}, f32[2,128,128]{2,1,0:T(8,128)S(1)}, f32[2,128,256]{2,1,0:T(8,128)S(1)}, s32[]{:T(128)}, ...), condition=%wide.region_19.20_spmd.clone, body=%wide.region_18.19_spmd.clone.sunk | while | flops 100925440 | bytes 1704055 | solution.py:295
  390.3 5.9 collective-permute-done.1
  401.1 6.2 collective-permute-done.1
  412.2 6.8 collective-permute-done.1
  423.9 6.8 collective-permute-done.1
  435.6 6.8 collective-permute-done.1
  447.2 6.8 collective-permute-done.1
  458.9 6.8 collective-permute-done.1
  470.0 38.6 %while.81 = (s32[]{:T(128)}, f32[2,128,256]{2,1,0:T(8,128)}, f32[8,2,128,128]{2,3,1,0:T(8,128)}, f32[8,2,128,256]{3,2,1,0:T(8,128)}, f32[8,2,128,256]{3,2,1,0:T(...) while((s32[]{:T(128)}, f32[2,128,256]{2,1,0:T(8,128)}, ...), condition=%wide.region_21.22_spmd, body=%wide.region_20.21_spmd.sunk | while | flops 201392128 | bytes 2623597 | solution.py:147
  508.6 3.4 convolution_add_fusion.7
  561.9 4.4 multiply_reduce_fusion.3
  574.4 6.4 pad_add_fusion
  596.0 3.8 convolution_convert_fusion.4
  608.3 3.5 convolution_convert_fusion.1
  628.2 38.6 %all-reduce.17 = (f32[4,1024]{1,0:T(4,128)S(1)}, f32[2]{0:T(128)}) all-reduce(f32[4,1024]{1,0:T(4,128)S(1)} %pad_add_fusion.2, f32[2]{0:T(128)S(1)} %neg.63), channel_id=1, replica_groups=mesh['seq'=8,'head'=4] {'seq'}, use_global_device_ids=true, to_apply=%region_44.46 | all-reduce | flops 4098 | bytes 32784 | tf_op jit(solution)/shard_map/psum | solution.py:332
  669.3 33.5 %reduce-scatter.33.cloned.1.call-done = bf16[128,2]{1,0:T(8,128)(2,1)} async-done(((bf16[1024,2]{1,0:T(8,128)(2,1)}), bf16[128,2]{1,0:T(8,128)(2,1)}) %reduce-scatter.33.cloned.1.call-update) | async-done | bytes 528
  704.3 52.1 %all-reduce.28.cloned.1.call-done = (bf16[512,1024]{1,0:T(8,128)(2,1)}, bf16[512,1024]{1,0:T(8,128)(2,1)}) async-done(((bf16[512,1024]{1,0:T(8,128)(2,1)}, bf16[512,1024]{1,0:T(8,128)(2,1)}), (bf16[512,1024]{1,0:T(8,128)(2,1)}, bf16[512,1024]{1,0:T(8,128)(2,1)})) %all-reduce.28.cloned.1.call-update) | async-done | bytes 2097168 | tf_op jit(solution)/shard_map/psum | solution.py:263
  758.6 21.7 %all-reduce.18 = (bf16[1024]{0:T(1024)(128)(2,1)S(1)}, bf16[256]{0:T(256)(128)(2,1)S(1)}, bf16[1024]{0:T(1024)(128)(2,1)S(1)}) all-reduce(bf16[1024]{0:T(1024)(128)(2,1)S(1)} %get-tuple-element.468, bf16[256]{0:T(256)(128)(2,1)S(1)} %copy-done.165, bf16[1024]{0:T(1024)(128)(2,1)S(1)} %copy-done.161), channel_id=2, replica_groups=mesh['seq'=8,'head'=4] {'seq'}, use_global_device_ids=true, to_apply=%region_33.35.clone | all-reduce | flops 2304 | bytes 9216
  780.4 6.0 psum.56
  787.0 34.9 %reduce-scatter.23.cloned.1.call-done = bf16[128,256]{1,0:T(8,128)(2,1)} async-done(((bf16[1024,256]{1,0:T(8,128)(2,1)}), bf16[128,256]{1,0:T(8,128)(2,1)}) %reduce-scatter.23.cloned.1.call-update) | async-done | bytes 65552 | tf_op jit(solution)/shard_map/reduce_scatter | solution.py:337
  823.4 62.8 %reduce-scatter.25.cloned.1.call-done = bf16[128,256]{1,0:T(8,128)(2,1)} async-done(((bf16[1024,256]{1,0:T(8,128)(2,1)}), bf16[128,256]{1,0:T(8,128)(2,1)}) %reduce-scatter.25.cloned.1.call-update) | async-done | bytes 65552 | tf_op jit(solution)/shard_map/reduce_scatter | solution.py:340
  888.9 4.2 fusion.49
  893.1 59.4 %reduce-scatter.35.cloned.1.call-done = bf16[128,512]{1,0:T(8,128)(2,1)} async-done(((bf16[1024,512]{1,0:T(8,128)(2,1)}), bf16[128,512]{1,0:T(8,128)(2,1)}) %reduce-scatter.35.cloned.1.call-update) | async-done | bytes 131088
  954.4 63.9 %reduce-scatter.29.cloned.1.call-done = bf16[128,512]{1,0:T(8,128)(2,1)} async-done(((bf16[1024,512]{1,0:T(8,128)(2,1)}), bf16[128,512]{1,0:T(8,128)(2,1)}) %reduce-scatter.29.cloned.1.call-update) | async-done | bytes 131088 | tf_op jit(solution)/shard_map/reduce_scatter | solution.py:346
  1019.9 64.5 %reduce-scatter.27.cloned.1.call-done = bf16[128,512]{1,0:T(8,128)(2,1)} async-done(((bf16[1024,512]{1,0:T(8,128)(2,1)}), bf16[128,512]{1,0:T(8,128)(2,1)}) %reduce-scatter.27.cloned.1.call-update) | async-done | bytes 131088 | tf_op jit(solution)/shard_map/reduce_scatter | solution.py:343
  1086.0 65.6 %reduce-scatter.37.cloned.1.call-done = bf16[128,704]{1,0:T(8,128)(2,1)} async-done(((bf16[1024,704]{1,0:T(8,128)(2,1)}), bf16[128,704]{1,0:T(8,128)(2,1)}) %reduce-scatter.37.cloned.1.call-update) | async-done | bytes 180240
  1153.5 65.6 %reduce-scatter.39.cloned.1.call-done = bf16[128,704]{1,0:T(8,128)(2,1)} async-done(((bf16[1024,704]{1,0:T(8,128)(2,1)}), bf16[128,704]{1,0:T(8,128)(2,1)}) %reduce-scatter.39.cloned.1.call-update) | async-done | bytes 180240
  1221.0 65.3 %reduce-scatter.41.cloned.1.call-done = bf16[128,704]{1,0:T(8,128)(2,1)} async-done(((bf16[1024,704]{1,0:T(8,128)(2,1)}), bf16[128,704]{1,0:T(8,128)(2,1)}) %reduce-scatter.41.cloned.1.call-update) | async-done | bytes 180240
  (723 shorter events, 372.2 us)
Async XLA Ops:
  7.2 296.1 %copy-start = (bf16[704,1024]{1,0:T(8,128)(2,1)S(1)}, bf16[704,1024]{1,0:T(8,128)(2,1)}, u32[]{:S(2)}) copy-start(bf16[704,1024]{1,0:T(8,128)(2,1)} %param.50) | copy-start | bytes 4325380
  7.2 289.3 %all-reduce.24.cloned.1.call-start = ((), (), s32[]{:S(2)}) async-start(), calls=%async_computation.10 | async-start | bytes 2097152 | tf_op jit(solution)/shard_map/psum | solution.py:255
  14.6 11.8 collective-permute-start.2
  20.2 17.1 %copy-start.74 = (f32[64,64]{1,0:T(8,128)}, f32[64,64]{1,0:T(8,128)S(1)}, u32[]{:S(2)}) copy-start(f32[64,64]{1,0:T(8,128)S(1)} %fusion.173) | copy-start | bytes 49156
  36.2 83.9 %copy-start.108 = (f32[8,2,64]{2,0,1:T(8,128)S(1)}, f32[8,2,64]{2,0,1:T(8,128)}, u32[]{:S(2)}) copy-start(f32[8,2,64]{2,0,1:T(8,128)} %get-tuple-element.574) | copy-start | bytes 12292
  36.2 83.9 %copy-start.117 = (f32[8,2,64]{2,0,1:T(8,128)S(1)}, f32[8,2,64]{2,0,1:T(8,128)}, u32[]{:S(2)}) copy-start(f32[8,2,64]{2,0,1:T(8,128)} %get-tuple-element.573) | copy-start | bytes 12292
  37.0 83.1 %copy-start.51 = (bf16[512,2,128]{2,0,1:T(8,128)(2,1)}, bf16[512,2,128]{2,0,1:T(8,128)(2,1)S(1)}, u32[]{:S(2)}) copy-start(bf16[512,2,128]{2,0,1:T(8,128)(2,1)S(1)} %multiply_convert_fusion.5) | copy-start | bytes 786436
  37.3 82.8 %copy-start.59 = (f32[8,2,64,64]{3,2,1,0:T(8,128)}, f32[8,2,64,64]{3,2,1,0:T(8,128)S(1)}, u32[]{:S(2)}) copy-start(f32[8,2,64,64]{3,2,1,0:T(8,128)S(1)} %fusion.170) | copy-start | bytes 786436
  153.3 5.9 collective-permute-start
  159.6 6.9 collective-permute-start
  166.9 7.8 collective-permute-start
  175.1 7.8 collective-permute-start
  183.2 8.4 collective-permute-start
  192.1 9.0 collective-permute-start
  201.5 7.5 collective-permute-start
  256.3 89.4 %all-reduce.26.cloned.1.call-start = ((), (), s32[]{:S(2)}) async-start(), calls=%async_computation.11 | async-start | bytes 2097152 | tf_op jit(solution)/shard_map/psum | solution.py:274
  309.0 358.9 %reduce-scatter.31.cloned.1.call-start = ((), (), s32[]{:S(2)}) async-start(), calls=%async_computation.16 | async-start | bytes 294912
  324.9 24.3 %copy-start.151 = (f32[512]{0:T(512)S(1)}, f32[512]{0:T(512)}, u32[]{:S(2)}) copy-start(f32[512]{0:T(512)} %copy-done.150) | copy-start | bytes 6148
  324.9 24.3 %copy-start.5 = (bf16[512,1024]{1,0:T(8,128)(2,1)S(1)}, bf16[512,1024]{1,0:T(8,128)(2,1)}, u32[]{:S(2)}) copy-start(bf16[512,1024]{1,0:T(8,128)(2,1)} %param.33) | copy-start | bytes 3145732
  324.9 24.3 %copy-start.124 = (f32[1024]{0:T(1024)S(1)}, f32[1024]{0:T(1024)}, u32[]{:S(2)}) copy-start(f32[1024]{0:T(1024)} %convert_element_type.255) | copy-start | bytes 12292
  324.9 24.3 %copy-start.146 = (f32[512]{0:T(512)S(1)}, f32[512]{0:T(512)}, u32[]{:S(2)}) copy-start(f32[512]{0:T(512)} %copy-done.145) | copy-start | bytes 6148
  324.9 24.4 %copy-start.169 = (f32[1,2,2,128]{3,1,2,0:T(2,128)S(1)}, f32[1,2,2,128]{3,1,2,0:T(2,128)}, u32[]{:S(2)}) copy-start(f32[1,2,2,128]{3,1,2,0:T(2,128)} %copy.348) | copy-start | bytes 6148
  361.3 157.7 %copy-start.11 = (f32[8,64,2,256]{3,1,2,0:T(8,128)}, f32[8,64,2,256]{3,1,2,0:T(8,128)S(1)}, u32[]{:S(2)}) copy-start(f32[8,64,2,256]{3,1,2,0:T(8,128)S(1)} %get-tuple-element.543) | copy-start | bytes 3145732
  389.0 7.2 collective-permute-start.1
  399.9 7.5 collective-permute-start.1
  410.9 8.1 collective-permute-start.1
  422.6 8.1 collective-permute-start.1
  434.3 8.1 collective-permute-start.1
  445.9 8.1 collective-permute-start.1
  457.6 8.1 collective-permute-start.1
  570.0 12.3 collective-permute-start.3
  574.3 128.5 %reduce-scatter.33.cloned.1.call-start = ((), (), s32[]{:S(2)}) async-start(), calls=%async_computation.17 | async-start | bytes 294912
  581.7 174.7 %all-reduce.28.cloned.1.call-start = ((), (), s32[]{:S(2)}) async-start(), calls=%async_computation.22 | async-start | bytes 4194304 | tf_op jit(solution)/shard_map/psum | solution.py:263
  590.2 231.7 %reduce-scatter.23.cloned.1.call-start = ((), (), s32[]{:S(2)}) async-start(), calls=%async_computation.12 | async-start | bytes 589824 | tf_op jit(solution)/shard_map/reduce_scatter | solution.py:337
  593.6 292.6 %reduce-scatter.25.cloned.1.call-start = ((), (), s32[]{:S(2)}) async-start(), calls=%async_computation.13 | async-start | bytes 589824 | tf_op jit(solution)/shard_map/reduce_scatter | solution.py:340
  595.9 356.6 %reduce-scatter.35.cloned.1.call-start = ((), (), s32[]{:S(2)}) async-start(), calls=%async_computation.18 | async-start | bytes 1179648
  602.2 416.0 %reduce-scatter.29.cloned.1.call-start = ((), (), s32[]{:S(2)}) async-start(), calls=%async_computation.15 | async-start | bytes 1179648 | tf_op jit(solution)/shard_map/reduce_scatter | solution.py:346
  605.1 479.3 %reduce-scatter.27.cloned.1.call-start = ((), (), s32[]{:S(2)}) async-start(), calls=%async_computation.14 | async-start | bytes 1179648 | tf_op jit(solution)/shard_map/reduce_scatter | solution.py:343
  608.0 543.7 %reduce-scatter.37.cloned.1.call-start = ((), (), s32[]{:S(2)}) async-start(), calls=%async_computation.19 | async-start | bytes 1769472
  614.4 604.7 %reduce-scatter.39.cloned.1.call-start = ((), (), s32[]{:S(2)}) async-start(), calls=%async_computation.20 | async-start | bytes 1769472
  620.3 666.0 %reduce-scatter.41.cloned.1.call-start = ((), (), s32[]{:S(2)}) async-start(), calls=%async_computation.21 | async-start | bytes 1769472
  623.5 132.9 %copy-start.121 = (f32[1024]{0:T(1024)S(1)}, f32[1024]{0:T(1024)}, u32[]{:S(2)}) copy-start(f32[1024]{0:T(1024)} %copy-done.120) | copy-start | bytes 12292
  623.5 132.9 %copy-start.140 = (f32[512]{0:T(512)S(1)}, f32[512]{0:T(512)}, u32[]{:S(2)}) copy-start(f32[512]{0:T(512)} %copy-done.139) | copy-start | bytes 6148
  626.1 132.5 %copy-start.161 = (bf16[1024]{0:T(1024)(128)(2,1)S(1)}, bf16[1024]{0:T(1024)(128)(2,1)}, u32[]{:S(2)}) copy-start(bf16[1024]{0:T(1024)(128)(2,1)} %get-tuple-element.464) | copy-start | bytes 6148
  626.1 132.5 %copy-start.165 = (bf16[256]{0:T(256)(128)(2,1)S(1)}, bf16[256]{0:T(256)(128)(2,1)}, u32[]{:S(2)}) copy-start(bf16[256]{0:T(256)(128)(2,1)} %get-tuple-element.466) | copy-start | bytes 1540
  626.1 262.8 %copy-start.149 = (f32[512]{0:T(512)S(1)}, f32[512]{0:T(512)}, u32[]{:S(2)}) copy-start(f32[512]{0:T(512)} %copy-done.148) | copy-start | bytes 6148
  756.3 132.5 %copy-start.70 = (bf16[512,1024]{1,0:T(8,128)(2,1)S(1)}, bf16[512,1024]{1,0:T(8,128)(2,1)}, u32[]{:S(2)}) copy-start(bf16[512,1024]{1,0:T(8,128)(2,1)} %get-tuple-element.540) | copy-start | bytes 3145732
  952.5 335.7 %copy-start.1 = (bf16[704,1024]{1,0:T(8,128)(2,1)S(1)}, bf16[704,1024]{1,0:T(8,128)(2,1)}, u32[]{:S(2)}) copy-start(bf16[704,1024]{1,0:T(8,128)(2,1)} %param.50) | copy-start | bytes 4325380
  (160 other events, 577.7 us)
Sparse Core Ops, SparseCore 0:
  256.4 40.0 all-reduce.23
  309.2 36.4 all-reduce.25
  574.4 64.3 reduce-scatter.30
  642.6 60.2 reduce-scatter.32
  705.7 50.5 all-reduce.27
  759.9 61.9 reduce-scatter.22
  825.2 60.9 reduce-scatter.24
  889.9 62.4 reduce-scatter.34
  955.9 62.2 reduce-scatter.28
  1021.9 62.4 reduce-scatter.26
  1087.8 63.8 reduce-scatter.36
  1155.3 63.7 reduce-scatter.38
  1222.5 63.7 reduce-scatter.40
where the time goes:
time: 1300 us; the launch traced here: 1290 us
  waiting for transfers between devices  693 us (53%)
  matrix products  203 us (16%)
  other arithmetic  161 us (12%)
  local copies, waits for them, and re-layouts  101 us (8%)
  blocking collectives  66.3 us (5%)
  starting transfers between devices  51.1 us (4%)
  between operations  17.7 us (1%)
    unnamed x19, waiting for transfers between devices  290 us
    another operation x5, other arithmetic, group_parts(): lax.linalg.triangular_solve(system, scaled_keys, left_side=True, lower=Tr...  80.6 us
    ppermute x16, waiting for transfers between devices, from_behind(): return lax.ppermute(block, axis, route)  65.6 us
    reduce_scatter x1, waiting for transfers between devices, per_device(): lax.psum_scatter(grad_wv.astype(jnp.bfloat16), 'seq', scatter_dimension=0...  64.5 us
    reduce_scatter x1, waiting for transfers between devices, per_device(): lax.psum_scatter(grad_wg.astype(jnp.bfloat16), 'seq', scatter_dimension=0...  63.9 us
    reduce_scatter x1, waiting for transfers between devices, per_device(): lax.psum_scatter(grad_wk.astype(jnp.bfloat16), 'seq', scatter_dimension=0...  62.8 us
    psum x1, waiting for transfers between devices, per_device(): lax.psum(matmul_bf(hidden, w_ffn_down).astype(jnp.bfloat16), 'head')  52.1 us
    ppermute x16, starting transfers between devices, from_behind(): return lax.ppermute(block, axis, route)  49.9 us
  transfers between devices with their start and end apart: 29, of which 27 were waited for; matrix products, arithmetic and copies ran while one was open for 7% of the time, Pallas kernels for 0%

commit v1 on v0

--- a/solution.py
+++ b/solution.py
@@ -16,6 +16,67 @@
     devices = range(lax.axis_size(axis))
     route = [(i - distance, i) for i in devices if i - distance in devices]
     return lax.ppermute(block, axis, route)
+
+
+def swap_with(block, axis, distance):
+    route = [(i, i ^ distance) for i in range(lax.axis_size(axis))]
+    return lax.ppermute(block, axis, route)
+
+
+def butterfly_sum(block, axis):
+    distance = 1
+    while distance < lax.axis_size(axis):
+        block = block + swap_with(block, axis, distance)
+        distance *= 2
+    return block
+
+
+def sum_over_heads(partial):
+    rows = partial.shape[0] // 2
+    odd = lax.axis_index("head") % 2 == 1
+    low, high = partial[:rows], partial[rows:]
+    own = jnp.where(odd, high, low).astype(jnp.float32)
+    own = own + swap_with(jnp.where(odd, low, high).astype(jnp.bfloat16), "head", 1).astype(jnp.float32)
+    distance = 2
+    while distance < lax.axis_size("head"):
+        sent = own.astype(jnp.bfloat16)
+        own = sent.astype(jnp.float32) + swap_with(sent, "head", distance).astype(jnp.float32)
+        distance *= 2
+    kept = own.astype(jnp.bfloat16)
+    other = swap_with(kept, "head", 1)
+    return jnp.concatenate(
+        [jnp.where(odd, other, kept), jnp.where(odd, kept, other)], axis=0
+    ).astype(jnp.float32)
+
+
+def exclusive_scan(transfer, offset, sign):
+    own_t, own_b = transfer, offset
+    send_t, send_b = transfer, offset
+    before_t = before_b = None
+    distance = 1
+    size = lax.axis_size("seq")
+
+    def product(a, b):
+        return jnp.einsum("hij,hjk->hik", a, b, precision=lax.Precision.HIGH)
+
+    while distance < size:
+        last = distance * 2 >= size
+        joined = send_b if last else jnp.concatenate([send_t, send_b], axis=2)
+        got = from_behind(joined.astype(jnp.bfloat16), "seq", sign * distance).astype(jnp.float32)
+        if last:
+            got_t, got_b = None, got
+        else:
+            got_t, got_b = got[..., :KEY], got[..., KEY:]
+        if before_t is None:
+            before_t, before_b = got_t, got_b
+        else:
+            before_b = before_b + product(before_t, got_b)
+            before_t = None if last else product(before_t, got_t)
+        if not last:
+            send_t = product(own_t, before_t)
+            send_b = product(own_t, before_b) + own_b
+        distance *= 2
+    return before_b
 
 
 def matmul_bf(first_operand, second_operand):
@@ -241,18 +302,11 @@
     parts, parts_back = jax.vjp(group_parts, keys_act, values_act, log_decay, beta_gate)
     transfer, offset_state = fold_maps(parts[5], parts[6], head_count)
 
-    def relay_step(turn_index, incoming_state):
-        following = (
-            jnp.einsum("hij,hjv->hiv", transfer, incoming_state, precision=highest_precision)
-            + offset_state
-        )
-        return from_behind(following.astype(jnp.bfloat16), "seq", 1).astype(following.dtype)
-
-    state_in = lax.fori_loop(0, lax.axis_size("seq") - 1, relay_step, jnp.zeros_like(offset_state))
+    state_in = exclusive_scan(transfer, offset_state, 1)
     mixer_result, mixer_back = jax.vjp(run_mixer, queries, parts, state_in)
     gated32, gate_back = jax.vjp(gate_norm, mixer_result[0], gate_pre, out_gain.astype(jnp.float32))
     gated = gated32.astype(jnp.bfloat16)
-    branch = lax.psum(matmul_bf(gated, w_out).astype(jnp.bfloat16), "head").astype(jnp.float32)
+    branch = sum_over_heads(matmul_bf(gated, w_out))
     middle = inputs32 + branch
     normed2_32, norm2_back = jax.vjp(row_norm, middle, norm2_gain.astype(jnp.float32))
     normed2 = normed2_32.astype(jnp.bfloat16)
@@ -264,35 +318,32 @@
         jnp.float32
     )
     layer_out = (middle + ffn_out).astype(jnp.bfloat16)
-    grad_down = inner_rows(hidden, cotangent)
+    grad_down = inner_rows(cotangent, hidden)
     grad_hidden = against_rows(cotangent, w_ffn_down)
     grad_fgate, grad_fup = swiglu_back(grad_hidden)
     grad_fgate = grad_fgate.astype(jnp.bfloat16)
     grad_fup = grad_fup.astype(jnp.bfloat16)
     grad_wfg = inner_rows(normed2, grad_fgate)
     grad_wfu = inner_rows(normed2, grad_fup)
-    grad_normed2 = lax.psum(
-        (against_rows(grad_fgate, w_ffn_gate) + against_rows(grad_fup, w_ffn_up)).astype(
-            jnp.bfloat16
-        ),
-        "head",
-    ).astype(jnp.float32)
+    grad_normed2 = sum_over_heads(
+        against_rows(grad_fgate, w_ffn_gate) + against_rows(grad_fup, w_ffn_up)
+    )
     grad_middle_n, grad_gain2 = norm2_back(grad_normed2)
     grad_middle = cotangent.astype(jnp.float32) + grad_middle_n
     grad_branch = grad_middle.astype(jnp.bfloat16)
-    grad_wout = inner_rows(gated, grad_branch)
+    grad_wout = inner_rows(grad_branch, gated)
+    early = lax.psum_scatter(
+        jnp.concatenate([grad_wfg, grad_wfu, grad_down, grad_wout], axis=1).astype(jnp.bfloat16),
+        "seq",
+        scatter_dimension=0,
+        tiled=True,
+    ).astype(jnp.float32)
     grad_gated = against_rows(grad_branch, w_out)
     grad_mixed, grad_gate_pre, grad_outgain = gate_back(grad_gated)
     direct = start_gradient(queries, parts, grad_mixed)
     flipped = jnp.swapaxes(transfer, 1, 2)
 
-    def relay_back(turn_index, pending):
-        following = (
-            jnp.einsum("hij,hjv->hiv", flipped, pending, precision=highest_precision) + direct
-        )
-        return from_behind(following.astype(jnp.bfloat16), "seq", -1).astype(following.dtype)
-
-    grad_state = lax.fori_loop(0, lax.axis_size("seq") - 1, relay_back, jnp.zeros_like(direct))
+    grad_state = exclusive_scan(flipped, direct, -1)
     grad_q, grad_parts, unused = mixer_back((grad_mixed, grad_state))
     grad_k, grad_v, grad_log, grad_beta = parts_back(grad_parts)
     grad_ext, grad_taps, grad_decay_pre, grad_beta_pre, grad_rate = prepare_back(
@@ -323,77 +374,61 @@
         + against_rows(grad_dp, w_decay)
         + against_rows(grad_bp, w_beta)
     )
-    grad_normed, grad_outgain_all = (
-        lax.psum(grad_normed_part.astype(jnp.bfloat16), "head").astype(jnp.float32),
-        lax.psum(grad_outgain.astype(jnp.bfloat16), "head").astype(jnp.float32),
-    )
+    late = lax.psum_scatter(
+        jnp.concatenate([grad_wq, grad_wk, grad_wv, grad_wg, grad_wd, grad_wb], axis=1).astype(
+            jnp.bfloat16
+        ),
+        "seq",
+        scatter_dimension=0,
+        tiled=True,
+    ).astype(jnp.float32)
+    grad_normed = sum_over_heads(grad_normed_part)
     grad_input_n, grad_gain1 = norm1_back(grad_normed)
     grad_input = grad_middle + grad_input_n
-    small_sums = lax.psum((grad_taps, grad_rate), "seq")
-    combined = (
-        lax.psum_scatter(
-            grad_gain1.astype(jnp.bfloat16), "seq", scatter_dimension=0, tiled=True
-        ).astype(jnp.float32),
-        lax.psum_scatter(
-            grad_wq.astype(jnp.bfloat16), "seq", scatter_dimension=0, tiled=True
-        ).astype(jnp.float32),
-        lax.psum_scatter(
-            grad_wk.astype(jnp.bfloat16), "seq", scatter_dimension=0, tiled=True
-        ).astype(jnp.float32),
-        lax.psum_scatter(
-            grad_wv.astype(jnp.bfloat16), "seq", scatter_dimension=0, tiled=True
-        ).astype(jnp.float32),
-        lax.psum_scatter(
-            grad_wg.astype(jnp.bfloat16), "seq", scatter_dimension=0, tiled=True
-        ).astype(jnp.float32),
-        lax.psum_scatter(
-            grad_wd.astype(jnp.bfloat16), "seq", scatter_dimension=0, tiled=True
-        ).astype(jnp.float32),
-        lax.psum_scatter(
-            grad_wb.astype(jnp.bfloat16), "seq", scatter_dimension=0, tiled=True
-        ).astype(jnp.float32),
-        lax.psum_scatter(
-            grad_outgain_all.astype(jnp.bfloat16), "seq", scatter_dimension=0, tiled=True
-        ).astype(jnp.float32),
-        lax.psum_scatter(
-            grad_wout.astype(jnp.bfloat16), "seq", scatter_dimension=1, tiled=True
-        ).astype(jnp.float32),
-        lax.psum_scatter(
-            grad_gain2.astype(jnp.bfloat16), "seq", scatter_dimension=0, tiled=True
-        ).astype(jnp.float32),
-        lax.psum_scatter(
-            grad_wfg.astype(jnp.bfloat16), "seq", scatter_dimension=0, tiled=True
-        ).astype(jnp.float32),
-        lax.psum_scatter(
-            grad_wfu.astype(jnp.bfloat16), "seq", scatter_dimension=0, tiled=True
-        ).astype(jnp.float32),
-        lax.psum_scatter(
-            grad_down.astype(jnp.bfloat16), "seq", scatter_dimension=1, tiled=True
-        ).astype(jnp.float32),
-    )
-    mixer_part = combined[:9]
-    ffn_part = combined[9:]
-    taps_sum = small_sums[0]
+    width = grad_gain1.shape[0]
+    small = jnp.concatenate(
+        [
+            grad_taps,
+            grad_gain2[None],
+            jnp.pad(jnp.concatenate([grad_outgain, grad_rate]), (0, width - VALUE - head_count))[None],
+        ],
+        axis=0,
+    )
+    small = butterfly_sum(small, "seq")
+    taps_sum = small[: conv_taps.shape[0]]
+    gain2_sum = small[conv_taps.shape[0]]
+    rate_sum = small[conv_taps.shape[0] + 1, VALUE : VALUE + head_count]
+    outgain_sum = butterfly_sum(small[conv_taps.shape[0] + 1, :VALUE], "head")
+    gain1_sum = butterfly_sum(grad_gain1, "seq")
+
+    def own_part(vec):
+        piece = vec.shape[0] // lax.axis_size("seq")
+        return lax.dynamic_slice(vec, (lax.axis_index("seq") * piece,), (piece,))
+
+    ff_cols = w_ffn_gate.shape[1]
+    value_cols = w_value.shape[1]
+    a = 2 * key_cols + value_cols
+    b = a + value_cols
     return (
         layer_out,
         grad_input,
-        mixer_part[0],
-        mixer_part[1],
-        mixer_part[2],
-        mixer_part[3],
-        mixer_part[4],
-        mixer_part[5],
-        mixer_part[6],
+        own_part(gain1_sum),
+        late[:, :key_cols],
+        late[:, key_cols : 2 * key_cols],
+        late[:, 2 * key_cols : a],
+        late[:, a:b],
+        late[:, b : b + head_count],
+        late[:, b + head_count :],
         taps_sum[:, :key_cols],
         taps_sum[:, key_cols : 2 * key_cols],
         taps_sum[:, 2 * key_cols :],
-        small_sums[1],
-        mixer_part[7],
-        mixer_part[8],
-        ffn_part[0],
-        ffn_part[1],
-        ffn_part[2],
-        ffn_part[3],
+        rate_sum,
+        own_part(outgain_sum),
+        early[:, 3 * ff_cols :].T,
+        own_part(gain2_sum),
+        early[:, :ff_cols],
+        early[:, ff_cols : 2 * ff_cols],
+        early[:, 2 * ff_cols : 3 * ff_cols].T,
     )
 
 

time: 1300 us -> 757 us (0.58)
  waiting for transfers between devices: 693 us -> 219 us
  blocking collectives: 66.3 us -> 0 us
  local copies, waits for them, and re-layouts: 101 us -> 131 us
  starting transfers between devices: 51.1 us -> 36.4 us
  other arithmetic: 161 us -> 148 us
    reduce_scatter x4 -> x0, waiting for transfers between devices: 226 us -> none  [the longest x1 64.5 us: per_device(): lax.psum_scatter(grad_wv.astype(jnp.bfloat16), 'seq', scatter_dimension=0...]
    unnamed x19 -> x5, waiting for transfers between devices: 290 us -> 98.4 us
    psum x2 -> x0, waiting for transfers between devices: 59.6 us -> none  [the longest x1 38.9 us: per_device(): lax.psum(matmul_bf(gated, w_out).astype(jnp.bfloat16), 'head')]
    ppermute x0 -> x17, waiting for transfers between devices: none -> 59.3 us  [swap_with(): return lax.ppermute(block, axis, route)]
    psum x2 -> x0, blocking collectives: 44.6 us -> none  [the longest x1 38.6 us: per_device(): small_sums = lax.psum((grad_taps, grad_rate), 'seq')]
    ppermute x16 -> x8, waiting for transfers between devices: 65.6 us -> 26.3 us  [from_behind(): return lax.ppermute(block, axis, route)]
    ppermute x16 -> x8, starting transfers between devices: 49.9 us -> 25.8 us  [from_behind(): return lax.ppermute(block, axis, route)]
    unnamed x1 -> x0, blocking collectives: 21.7 us -> none
  transfers between devices with their start and end apart: 29 -> 28, of which waited for: 27 -> 20; matrix products, arithmetic and copies ran while one was open for 7% -> 11% of each run, Pallas kernels for 0% -> 0%
where the time goes in v1:
time: 757 us; the launch traced here: 750 us
  waiting for transfers between devices  219 us (29%)
  matrix products  197 us (26%)
  other arithmetic  148 us (20%)
  local copies, waits for them, and re-layouts  131 us (17%)
  starting transfers between devices  36.4 us (5%)
  between operations  16.7 us (2%)
    unnamed x5, waiting for transfers between devices  98.4 us
    another operation x5, other arithmetic, group_parts(): lax.linalg.triangular_solve(system, scaled_keys, left_side=True, lower=Tr...  81.2 us
    ppermute x17, waiting for transfers between devices, swap_with(): return lax.ppermute(block, axis, route)  59.3 us
    dot_general x24, matrix products, carry_step(): jnp.einsum('hij,hjv->hiv', table_entries[0], incoming_state, precision=hi...  43.8 us
    psum x1, waiting for transfers between devices, per_device(): lax.psum(matmul_bf(hidden, w_ffn_down).astype(jnp.bfloat16), 'head')  35 us
    unnamed x387, local copies, waits for them, and re-layouts  34 us
    ppermute x8, waiting for transfers between devices, from_behind(): return lax.ppermute(block, axis, route)  26.3 us
    ppermute x8, starting transfers between devices, from_behind(): return lax.ppermute(block, axis, route)  25.8 us
  transfers between devices with their start and end apart: 28, of which 20 were waited for; matrix products, arithmetic and copies ran while one was open for 11% of the time, Pallas kernels for 0%

profile of v1, /device:TPU:0, one launch (start us, length us, event | category | flops | bytes accessed | tf_op | source)
XLA Modules:
  0.0 750.0 jit_solution(8466255008071230220)
XLA Ops:
  14.2 5.7 collective-permute-start
  28.3 3.5 fusion.43
  38.0 80.0 %custom-call.12 = f32[8,2,1,64,64]{3,4,2,1,0:T(8,128)} custom-call(f32[8,2,1,64,64]{4,3,2,1,0:T(8,128)} %add_bitcast_fusion), custom_call_target="InvertDiagBlocksLowerTriangular" | custom-call | tf_op jit(solution)/shard_map/jvp()/triangular_solve | solution.py:155
  120.1 2.5 fusion.76
  124.9 3.3 fusion.115
  128.2 2.9 convolution_subtract_fusion.1
  131.1 21.3 %while.60 = (s32[]{:T(128)}, f32[2,128,128]{2,1,0:T(8,128)S(1)}, f32[2,128,256]{2,1,0:T(8,128)S(1)}, f32[8,2,128,128]{3,2,1,0:T(8,128)}, f32[8,2,128,256]{3,2,1,0:T(8,128)}, /*index=5*/s32[]{:T(128)}, s32[]{:T(128)}) while((s32[]{:T(128)}, f32[2,128,128]{2,1,0:T(8,128)S(1)}, f32[2,128,256]{2,1,0:T(8,128)S(1)}, ...), condition=%wide.region_3.4_spmd.clone, body=%wide.region_2.3_spmd.clone.sunk | while | flops 151126016 | bytes 2098786 | solution.py:189
  153.3 3.4 collective-permute-start.1
  164.0 5.6 collective-permute-start.2
  175.1 5.4 collective-permute-start.3
  185.9 17.7 %while.58 = (s32[]{:T(128)}, f32[2,128,256]{2,1,0:T(8,128)S(1)}, f32[8,2,128,256]{3,2,1,0:T(8,128)}, f32[8,2,128,128]{3,2,1,0:T(8,128)}, f32[8,2,128,256]{3,2,1,0:T(8,128)}, /*index=5*/s32[]{:T(128)}) while((s32[]{:T(128)}, f32[2,128,256]{2,1,0:T(8,128)S(1)}, f32[8,2,128,256]{3,2,1,0:T(8,128)}, f32[8,2,128,128]{3,2,1,0:T(8,128)}, ...), condition=%wide.region_5.6_spmd, body=%wide.region_4.5_spmd.sunk | while | flops 100728832 | bytes 1967185 | solution.py:208
  203.6 3.3 convolution_subtract_fusion.2
  214.3 3.4 multiply_convert_fusion.3
  222.5 12.5 %collective-permute-done.5 = bf16[256,1024]{1,0:T(8,128)(2,1)S(1)} collective-permute-done((bf16[256,1024]{1,0:T(8,128)(2,1)S(1)}, bf16[256,1024]{1,0:T(8,128)(2,1)S(1)}, u32[]{:S(2)}, u32[]{:S(2)}) %collective-permute-start.5) | collective-permute-done | bytes 524320 | tf_op jit(solution)/shard_map/ppermute | solution.py:23
  240.8 2.4 multiply_convert_fusion.1
  249.5 12.7 %collective-permute-done.8 = bf16[256,1024]{1,0:T(8,128)(2,1)S(1)} collective-permute-done((bf16[256,1024]{1,0:T(8,128)(2,1)S(1)}, bf16[256,1024]{1,0:T(8,128)(2,1)S(1)}, u32[]{:S(2)}, u32[]{:S(2)}) %collective-permute-start.8) | collective-permute-done | bytes 524320 | tf_op jit(solution)/shard_map/ppermute | solution.py:23
  266.5 2.9 reshape.338
  269.4 3.3 convolution_convert_fusion.3
  276.6 35.0 %all-reduce.17.cloned.1.call-done = bf16[512,1024]{1,0:T(8,128)(2,1)} async-done(((bf16[512,1024]{1,0:T(8,128)(2,1)}), bf16[512,1024]{1,0:T(8,128)(2,1)}) %all-reduce.17.cloned.1.call-update) | async-done | bytes 1048592 | tf_op jit(solution)/shard_map/psum | solution.py:317
  311.5 3.9 fusion.36
  317.7 3.0 reshape.337
  320.6 2.9 multiply_reduce_fusion.6
  327.2 2.6 fusion.70
  331.9 3.3 convolution_subtract_fusion
  335.2 24.6 %while.61 = (s32[]{:T(128)}, f32[2,128,256]{2,1,0:T(8,128)}, f32[8,2,128,256]{3,2,1,0:T(8,128)}, f32[8,2,128,128]{2,3,1,0:T(8,128)}, s32[]{:T(128)}, /*index=5*/s32[]{:T(128)}, s32[]{:T(128)}) while((s32[]{:T(128)}, f32[2,128,256]{2,1,0:T(8,128)}, f32[8,2,128,256]{3,2,1,0:T(8,128)}, f32[8,2,128,128]{2,3,1,0:T(8,128)}, ...), condition=%wide.region_13.14_spmd.clone, body=%wide.region_12.13_spmd.clone.sunk | while | flops 100794368 | bytes 1443434 | solution.py:243
  362.5 5.4 convolution_add_fusion.4
  367.9 3.1 fusion.80
  377.6 2.8 convolution_convert_fusion.6
  380.4 5.6 collective-permute-done.11
  388.0 7.9 %collective-permute-done.12 = bf16[2,128,256]{2,1,0:T(8,128)(2,1)S(1)} collective-permute-done((bf16[2,128,256]{2,1,0:T(8,128)(2,1)S(1)}, bf16[2,128,256]{2,1,0:T(8,128)(2,1)S(1)}, u32[]{:S(2)}, u32[]{:S(2)}) %collective-permute-start.12) | collective-permute-done | bytes 131104 | tf_op jit(solution)/shard_map/ppermute | solution.py:18
  399.7 46.4 %while.59 = (s32[]{:T(128)}, f32[2,128,256]{2,1,0:T(8,128)}, f32[8,2,128,128]{2,3,1,0:T(8,128)}, f32[8,2,128,256]{3,2,1,0:T(8,128)}, f32[8,2,128,256]{3,2,1,0:T(...) while((s32[]{:T(128)}, f32[2,128,256]{2,1,0:T(8,128)}, ...), condition=%wide.region_15.16_spmd, body=%wide.region_14.15_spmd.sunk | while | flops 201392128 | bytes 2623605 | solution.py:208
  446.1 5.1 fusion.250
  459.0 2.5 copy.370
  463.9 2.5 fusion.252
  489.4 4.9 broadcast_multiply_fusion.5
  495.8 2.4 copy.430
  506.9 4.9 multiply_reduce_fusion.3
  517.1 9.1 %collective-permute-done.13 = f32[3,1024]{0,1:T(8,128)S(1)} collective-permute-done((f32[3,1024]{0,1:T(8,128)S(1)}, f32[3,1024]{0,1:T(8,128)S(1)}, u32[]{:S(2)}, u32[]{:S(2)}) %collective-permute-start.13) | collective-permute-done | bytes 12320 | tf_op jit(solution)/shard_map/ppermute | solution.py:18
  531.0 17.2 %concatenate.62 = bf16[1024,1540]{0,1:T(8,128)(2,1)} concatenate(bf16[1024,256]{0,1:T(8,128)(2,1)} %convolution_convert_fusion.8, bf16[1024,256]{0,1:T(8,128)(2,1)} %convolution_convert_fusion.7, bf16[1024,512]{0,1:T(8,128)(2,1)} %convolution_convert_fusion.4, bf16[1024,512]{0,1:T(8,128)(2,1)} %convolution_convert_fusion.6, bf16[1024,2]{0,1:T(2,128)(2,1)S(1)} %convolution_convert_fusion.15, ...), dimensions={1} | concatenate | bytes 6307840 | tf_op jit(solution)/shard_map/concatenate | solution.py:378
  548.3 5.4 copy.433
  561.1 14.9 %pad_maximum_fusion = bf16[1024,2624]{0,1:T(8,128)(2,1)} fusion(bf16[1024,512]{0,1:T(8,128)(2,1)S(1)} %convolution_convert_fusion.5, bf16[1024,704]{0,1:T(8,128)(2,1)S(1)} %fusion.44, bf16[1024,704]{0,1:T(8,128)(2,1)S(1)} %convolution_convert_fusion, bf16[1024,704]{0,1:T(8,128)(2,1)S(1)} %convolution_convert_fusion.1), kind=kLoop, calls=%fused_computation.35 | loop fusion | flops 21495808 | bytes 10747904 | tf_op jit(solution)/shard_map/concatenate | solution.py:336
  576.0 8.1 %copy.435 = bf16[1024,2624]{1,0:T(8,128)(2,1)} copy(bf16[1024,2624]{0,1:T(8,128)(2,1)} %pad_maximum_fusion) | data formatting | bytes 10747904
  596.5 10.5 %collective-permute-done.15 = bf16[256,1024]{1,0:T(8,128)(2,1)S(1)} collective-permute-done((bf16[256,1024]{1,0:T(8,128)(2,1)S(1)}, bf16[256,1024]{1,0:T(8,128)(2,1)S(1)}, u32[]{:S(2)}, u32[]{:S(2)}) %collective-permute-start.15) | collective-permute-done | bytes 524320 | tf_op jit(solution)/shard_map/ppermute | solution.py:23
  608.1 3.9 collective-permute-done.21
  612.0 6.4 collective-permute-done.22
  627.7 3.6 collective-permute-done.18
  633.2 2.6 collective-permute-done.19
  641.5 98.4 %reduce-scatter.9.cloned.1.call-done = bf16[128,2624]{1,0:T(8,128)(2,1)} async-done(((bf16[1024,2624]{1,0:T(8,128)(2,1)}), bf16[128,2624]{1,0:T(8,128)(2,1)}) %reduce-scatter.9.cloned.1.call-update) | async-done | bytes 671760
  (733 shorter events, 300.9 us)
Async XLA Ops:
  7.2 233.6 %copy-start = (bf16[1024,704]{0,1:T(8,128)(2,1)S(1)}, bf16[1024,704]{0,1:T(8,128)(2,1)}, u32[]{:S(2)}) copy-start(bf16[1024,704]{0,1:T(8,128)(2,1)} %param.44) | copy-start | bytes 4325380
  7.2 304.3 %all-reduce.17.cloned.1.call-start = ((), (), s32[]{:S(2)}) async-start(), calls=%async_computation.2 | async-start | bytes 2097152 | tf_op jit(solution)/shard_map/psum | solution.py:317
  14.2 12.4 %collective-permute-start = (bf16[3,1024]{0,1:T(8,128)(2,1)}, bf16[3,1024]{0,1:T(8,128)(2,1)}, u32[]{:S(2)}, u32[]{:S(2)}) collective-permute-start(bf16[3,1024]{0,1:T(8,128)(2,1)} %pad_maximum_fusion.4), channel_id=1, source_target_pairs={{0,4},{4,8},{8,12},{12,16},{16,20},{20,24},{24,28},{1,5},{5,9},{9,... | collective-permute-start | bytes 18440 | tf_op jit(solution)/shard_map/ppermute | solution.py:18
  19.9 16.9 %copy-start.103 = (f32[64,64]{1,0:T(8,128)}, f32[64,64]{1,0:T(8,128)S(1)}, u32[]{:S(2)}) copy-start(f32[64,64]{1,0:T(8,128)S(1)} %fusion.192) | copy-start | bytes 49156
  20.0 16.9 %copy-start.69 = (f32[64,64]{1,0:T(8,128)}, f32[64,64]{1,0:T(8,128)S(1)}, u32[]{:S(2)}) copy-start(f32[64,64]{1,0:T(8,128)S(1)} %fusion.186) | copy-start | bytes 49156
  35.8 82.3 %copy-start.139 = (f32[512,2]{0,1:T(2,128)}, f32[512,2]{0,1:T(2,128)S(1)}, u32[]{:S(2)}) copy-start(f32[512,2]{0,1:T(2,128)S(1)} %add_rsqrt_fusion.1) | copy-start | bytes 12292
  36.6 81.5 %copy-start.48 = (bf16[512,2,128]{2,0,1:T(8,128)(2,1)}, bf16[512,2,128]{2,0,1:T(8,128)(2,1)S(1)}, u32[]{:S(2)}) copy-start(bf16[512,2,128]{2,0,1:T(8,128)(2,1)S(1)} %multiply_convert_fusion.5) | copy-start | bytes 786436
  36.9 81.2 %copy-start.58 = (f32[8,2,64,64]{3,2,1,0:T(8,128)}, f32[8,2,64,64]{3,2,1,0:T(8,128)S(1)}, u32[]{:S(2)}) copy-start(f32[8,2,64,64]{3,2,1,0:T(8,128)S(1)} %fusion.165) | copy-start | bytes 786436
  131.1 27.7 %copy-start.142 = (f32[512,2]{0,1:T(2,128)S(1)}, f32[512,2]{0,1:T(2,128)}, u32[]{:S(2)}) copy-start(f32[512,2]{0,1:T(2,128)} %get-tuple-element.490) | copy-start | bytes 12292
  152.3 21.6 %copy-start.14 = (f32[2,128,128]{2,1,0:T(8,128)}, f32[2,128,128]{2,1,0:T(8,128)S(1)}, u32[]{:S(2)}) copy-start(f32[2,128,128]{2,1,0:T(8,128)S(1)} %get-tuple-element.301) | copy-start | bytes 393220
  152.4 17.3 %copy-start.50 = (bf16[512,2,128]{2,0,1:T(8,128)(2,1)S(1)}, bf16[512,2,128]{2,0,1:T(8,128)(2,1)}, u32[]{:S(2)}) copy-start(bf16[512,2,128]{2,0,1:T(8,128)(2,1)} %copy-done.48) | copy-start | bytes 786436
  153.3 6.9 collective-permute-start.1
  160.0 23.0 %copy-start.52 = (bf16[512,2,128]{2,0,1:T(8,128)(2,1)}, bf16[512,2,128]{2,0,1:T(8,128)(2,1)S(1)}, u32[]{:S(2)}) copy-start(bf16[512,2,128]{2,0,1:T(8,128)(2,1)S(1)} %multiply_convert_fusion.4) | copy-start | bytes 786436
  164.0 8.8 %collective-permute-start.2 = (bf16[2,128,384]{2,1,0:T(8,128)(2,1)S(1)}, bf16[2,128,384]{2,1,0:T(8,128)(2,1)S(1)}, u32[]{:S(2)}, u32[]{:S(2)}) collective-permute-start(bf16[2,128,384]{2,1,0:T(8,128)(2,1)S(1)} %pad_maximum_fusion.7), channel_id=1, source_target_pairs={{0,8},{4,12},{8,16},{12,20},{16,24},{20,28},{1,9},{5,13},{9,17},{1... | collective-permute-start | bytes 589832 | tf_op jit(solution)/shard_map/ppermute | solution.py:18
  175.1 7.9 %collective-permute-start.3 = (bf16[2,128,256]{2,1,0:T(8,128)(2,1)S(1)}, bf16[2,128,256]{2,1,0:T(8,128)(2,1)S(1)}, u32[]{:S(2)}, u32[]{:S(2)}) collective-permute-start(bf16[2,128,256]{2,1,0:T(8,128)(2,1)S(1)} %fusion.60), channel_id=1, source_target_pairs={{0,16},{4,20},{8,24},{12,28},{1,17},{5,21},{9,25},{13,29},{2,18},{... | collective-permute-start | bytes 393224 | tf_op jit(solution)/shard_map/ppermute | solution.py:18
  185.9 17.7 %copy-start.10 = (f32[8,2,64,128]{3,2,1,0:T(8,128)S(1)}, f32[8,2,64,128]{3,2,1,0:T(8,128)}, u32[]{:S(2)}) copy-start(f32[8,2,64,128]{3,2,1,0:T(8,128)} %copy-done.9) | copy-start | bytes 1572868
  218.7 2.0 collective-permute-start.4
  220.9 14.0 %collective-permute-start.5 = (bf16[256,1024]{1,0:T(8,128)(2,1)S(1)}, bf16[256,1024]{1,0:T(8,128)(2,1)S(1)}, u32[]{:S(2)}, u32[]{:S(2)}) collective-permute-start(bf16[256,1024]{1,0:T(8,128)(2,1)S(1)} %add_convert_fusion.6), channel_id=1, source_target_pairs={{0,2},{1,3},{2,0},{3,1},{4,6},{5,7},{6,4},{7,5},{8,10},{9,11},{10,... | collective-permute-start | bytes 1572872 | tf_op jit(solution)/shard_map/ppermute | solution.py:23
  235.1 2.0 collective-permute-start.6
  245.5 17.7 %copy-start.106 = (f32[8,64,2]{1,0,2:T(8,128)S(1)}, f32[8,64,2]{1,0,2:T(8,128)}, u32[]{:S(2)}) copy-start(f32[8,64,2]{1,0,2:T(8,128)} %copy-done.105) | copy-start | bytes 12292
  245.5 18.3 %copy-start.123 = (f32[8,2,64]{2,0,1:T(8,128)S(1)}, f32[8,2,64]{2,0,1:T(8,128)}, u32[]{:S(2)}) copy-start(f32[8,2,64]{2,0,1:T(8,128)} %get-tuple-element.584) | copy-start | bytes 12292
  245.5 18.9 %copy-start.113 = (f32[8,2,64]{2,0,1:T(8,128)S(1)}, f32[8,2,64]{2,0,1:T(8,128)}, u32[]{:S(2)}) copy-start(f32[8,2,64]{2,0,1:T(8,128)} %get-tuple-element.585) | copy-start | bytes 12292
  245.6 19.5 %copy-start.33 = (f32[8,2,128,128]{3,2,1,0:T(8,128)S(1)}, f32[8,2,128,128]{3,2,1,0:T(8,128)}, u32[]{:S(2)}) copy-start(f32[8,2,128,128]{3,2,1,0:T(8,128)} %get-tuple-element.826) | copy-start | bytes 3145732
  245.6 2.1 collective-permute-start.7
  247.9 18.5 %copy-start.102 = (bf16[2,128,128]{1,2,0:T(8,128)(2,1)S(1)}, bf16[2,128,128]{1,2,0:T(8,128)(2,1)}, u32[]{:S(2)}) copy-start(bf16[2,128,128]{1,2,0:T(8,128)(2,1)} %copy-done.101) | copy-start | bytes 196612
  247.9 18.6 %copy-start.122 = (f32[8,64,2]{1,0,2:T(8,128)S(1)}, f32[8,64,2]{1,0,2:T(8,128)}, u32[]{:S(2)}) copy-start(f32[8,64,2]{1,0,2:T(8,128)} %copy-done.121) | copy-start | bytes 12292
  247.9 14.3 %collective-permute-start.8 = (bf16[256,1024]{1,0:T(8,128)(2,1)S(1)}, bf16[256,1024]{1,0:T(8,128)(2,1)S(1)}, u32[]{:S(2)}, u32[]{:S(2)}) collective-permute-start(bf16[256,1024]{1,0:T(8,128)(2,1)S(1)} %add_convert_fusion.4), channel_id=1, source_target_pairs={{0,2},{1,3},{2,0},{3,1},{4,6},{5,7},{6,4},{7,5},{8,10},{9,11},{10,... | collective-permute-start | bytes 1572872 | tf_op jit(solution)/shard_map/ppermute | solution.py:23
  263.2 9.6 %collective-permute-start.9 = (bf16[256,1024]{1,0:T(8,128)(2,1)}, bf16[256,1024]{1,0:T(8,128)(2,1)}, u32[]{:S(2)}, u32[]{:S(2)}) collective-permute-start(bf16[256,1024]{1,0:T(8,128)(2,1)} %add_convert_fusion.3), channel_id=1, source_target_pairs={{0,1},{1,0},{2,3},{3,2},{4,5},{5,4},{6,7},{7,6},{8,9},{9,8},{10,11... | collective-permute-start | bytes 1572872 | tf_op jit(solution)/shard_map/ppermute | solution.py:23
  272.8 363.6 %reduce-scatter.7.cloned.1.call-start = ((), (), s32[]{:S(2)}) async-start(), calls=%async_computation.3 | async-start | bytes 3833856
  276.6 38.9 %copy-start.177 = (f32[1,2,2,128]{3,1,2,0:T(2,128)S(1)}, f32[1,2,2,128]{3,1,2,0:T(2,128)}, u32[]{:S(2)}) copy-start(f32[1,2,2,128]{3,1,2,0:T(2,128)} %copy.444) | copy-start | bytes 6148
  361.0 10.1 %collective-permute-start.10 = (bf16[2,128,384]{1,2,0:T(8,128)(2,1)S(1)}, bf16[2,128,384]{1,2,0:T(8,128)(2,1)S(1)}, u32[]{:S(2)}, u32[]{:S(2)}) collective-permute-start(bf16[2,128,384]{1,2,0:T(8,128)(2,1)S(1)} %pad_maximum_fusion.8), channel_id=1, source_target_pairs={{4,0},{8,4},{12,8},{16,12},{20,16},{24,20},{28,24},{5,1},{9,5},{13... | collective-permute-start | bytes 589832 | tf_op jit(solution)/shard_map/ppermute | solution.py:18
  376.3 9.6 %collective-permute-start.11 = (bf16[2,128,384]{2,1,0:T(8,128)(2,1)S(1)}, bf16[2,128,384]{2,1,0:T(8,128)(2,1)S(1)}, u32[]{:S(2)}, u32[]{:S(2)}) collective-permute-start(bf16[2,128,384]{2,1,0:T(8,128)(2,1)S(1)} %pad_maximum_fusion.9), channel_id=1, source_target_pairs={{8,0},{12,4},{16,8},{20,12},{24,16},{28,20},{9,1},{13,5},{17,9},{2... | collective-permute-start | bytes 589832 | tf_op jit(solution)/shard_map/ppermute | solution.py:18
  386.5 9.5 %collective-permute-start.12 = (bf16[2,128,256]{2,1,0:T(8,128)(2,1)S(1)}, bf16[2,128,256]{2,1,0:T(8,128)(2,1)S(1)}, u32[]{:S(2)}, u32[]{:S(2)}) collective-permute-start(bf16[2,128,256]{2,1,0:T(8,128)(2,1)S(1)} %fusion.62), channel_id=1, source_target_pairs={{16,0},{20,4},{24,8},{28,12},{17,1},{21,5},{25,9},{29,13},{18,2},{... | collective-permute-start | bytes 393224 | tf_op jit(solution)/shard_map/ppermute | solution.py:18
  513.0 13.3 %collective-permute-start.13 = (f32[3,1024]{0,1:T(8,128)S(1)}, f32[3,1024]{0,1:T(8,128)S(1)}, u32[]{:S(2)}, u32[]{:S(2)}) collective-permute-start(f32[3,1024]{0,1:T(8,128)S(1)} %pad_add_fusion.1), channel_id=1, source_target_pairs={{4,0},{8,4},{12,8},{16,12},{20,16},{24,20},{28,24},{5,1},{9,5},{13... | collective-permute-start | bytes 36872 | tf_op jit(solution)/shard_map/ppermute | solution.py:18
  553.7 186.2 %reduce-scatter.9.cloned.1.call-start = ((), (), s32[]{:S(2)}) async-start(), calls=%async_computation.4 | async-start | bytes 6193152
  590.6 2.0 collective-permute-start.14
  592.9 30.2 %copy-start.129 = (f32[1024]{0:T(1024)S(1)}, f32[1024]{0:T(1024)}, u32[]{:S(2)}) copy-start(f32[1024]{0:T(1024)} %copy-done.128) | copy-start | bytes 12292
  592.9 30.2 %copy-start.151 = (f32[512]{0:T(512)S(1)}, f32[512]{0:T(512)}, u32[]{:S(2)}) copy-start(f32[512]{0:T(512)} %copy-done.150) | copy-start | bytes 6148
  592.9 14.1 %collective-permute-start.15 = (bf16[256,1024]{1,0:T(8,128)(2,1)S(1)}, bf16[256,1024]{1,0:T(8,128)(2,1)S(1)}, u32[]{:S(2)}, u32[]{:S(2)}) collective-permute-start(bf16[256,1024]{1,0:T(8,128)(2,1)S(1)} %add_convert_fusion.2), channel_id=1, source_target_pairs={{0,2},{1,3},{2,0},{3,1},{4,6},{5,7},{6,4},{7,5},{8,10},{9,11},{10,... | collective-permute-start | bytes 1572872 | tf_op jit(solution)/shard_map/ppermute | solution.py:23
  595.1 13.0 %collective-permute-start.20 = (f32[6,1024]{1,0:T(8,128)S(1)}, f32[6,1024]{1,0:T(8,128)S(1)}, u32[]{:S(2)}, u32[]{:S(2)}) collective-permute-start(f32[6,1024]{1,0:T(8,128)S(1)} %pad_maximum_fusion.10), channel_id=1, source_target_pairs={{0,4},{4,0},{8,12},{12,8},{16,20},{20,16},{24,28},{28,24},{1,5},{5... | collective-permute-start | bytes 73736 | tf_op jit(solution)/shard_map/ppermute | solution.py:23
  608.0 13.8 %collective-permute-start.16 = (bf16[256,1024]{1,0:T(8,128)(2,1)}, bf16[256,1024]{1,0:T(8,128)(2,1)}, u32[]{:S(2)}, u32[]{:S(2)}) collective-permute-start(bf16[256,1024]{1,0:T(8,128)(2,1)} %add_convert_fusion.1), channel_id=1, source_target_pairs={{0,1},{1,0},{2,3},{3,2},{4,5},{5,4},{6,7},{7,6},{8,9},{9,8},{10,11... | collective-permute-start | bytes 1572872 | tf_op jit(solution)/shard_map/ppermute | solution.py:23
  608.0 4.0 collective-permute-start.21
  612.0 6.4 collective-permute-start.22
  618.4 1.2 collective-permute-start.23
  619.6 6.5 collective-permute-start.24
  624.0 3.7 collective-permute-start.17
  627.7 3.6 collective-permute-start.18
  631.3 4.5 collective-permute-start.19
  (167 other events, 620.4 us)
Sparse Core Ops, SparseCore 0:
  272.9 38.5 all-reduce.16
  553.8 77.1 reduce-scatter.6
  634.6 105.1 reduce-scatter.8
